TPU v7x, 256 devices: a whole 4x4x8 slice. The times are simulated.
256 devices in a mesh: var: 32 (over z, y_lo, core), samp: 8 (over y_hi, x).
Axes of the slice: x: 4, y: 4 (y_hi: 2, y_lo: 2; y = y_hi * 2 + y_lo), z: 8, core: 2. Of those that a mesh axis runs over, the one named last changes fastest.
Arguments:
- dosage: float32 [4096, 8192], P('samp', 'var'), may hold values from 0 to 2, as said below
Outputs:
- ld_stat: float32 [8192, 4096], P('var', 'samp')
Inputs may be any that keep to these rules, and one draw needn't show every extreme that they name: `dosage`: dosages of imputed biallelic variants.
All inputs are finite; a program needn't handle non-finite values.
Results may differ from a plain program's by a relative error of at most 0.0003.
Values sent between devices are 32-bit elements; how exact they have to be, the bound alone decides.
A program may use at most 64 MiB of HBM per device.

v0:
```python
import jax
import jax.numpy as jnp
from jax import lax
from jax.sharding import PartitionSpec as P

BAND = 4096


def shifted(block, axis, distance):
    devices = range(lax.axis_size(axis))
    route = [(i - distance, i) for i in devices if i - distance in devices]
    return lax.ppermute(block, axis, route)


def gram_tile(left, right):
    return lax.dot_general(
        left,
        right,
        (((0,), (0,)), ((), ())),
        precision=lax.Precision.HIGHEST,
        preferred_element_type=jnp.float32,
    )


def skew_tile(tile):
    width = tile.shape[0]
    padded = jnp.pad(tile, ((0, 0), (width, width)))
    flattened = jnp.pad(padded.reshape(-1), (0, width))
    return flattened.reshape(width, 3 * width + 1)[:, 1 : 1 + 2 * width]


def body(dosage):
    samples_all = dosage.shape[0] * lax.axis_size("samp")
    allele_total, allele_square = lax.psum(
        (jnp.sum(dosage, axis=0), jnp.sum(dosage * dosage, axis=0)), "samp"
    )
    mean_dose = allele_total / samples_all
    inv_scale = lax.rsqrt(allele_square / samples_all - mean_dose * mean_dose + 1e-06)
    standard = (dosage - mean_dose) * inv_scale
    block_width = standard.shape[1]
    span_blocks = BAND // block_width
    holder = jnp.zeros((block_width, (span_blocks + 2) * block_width), jnp.float32)
    holder = holder.at[:, 0 : 2 * block_width].add(skew_tile(gram_tile(standard, standard)))
    for distance in range(1, span_blocks + 1):
        arrived = shifted(standard, "var", -distance)
        first = distance * block_width
        holder = holder.at[:, first : first + 2 * block_width].add(
            skew_tile(gram_tile(standard, arrived))
        )
    band_part = holder[:, block_width : block_width + BAND]
    summed = lax.psum_scatter(band_part, "samp", scatter_dimension=1, tiled=True)
    return summed * (1.0 / jnp.sqrt(jnp.float32(samples_all)))


def solution(mesh):
    placed = (P("samp", "var"),)
    return jax.shard_map(
        body, mesh=mesh, in_specs=placed, out_specs=P("var", "samp"), check_vma=False
    )
```

profile of v0, /device:TPU:2, one launch (start us, length us, event | category | flops | bytes accessed | tf_op | source)
XLA Modules:
  0.0 538.7 jit_solution(18081169721483911103)
XLA Ops:
  7.7 21.2 %all-reduce.35 = (f32[256]{0:T(256)S(1)}, f32[256]{0:T(256)S(1)}) all-reduce(f32[256]{0:T(256)S(1)} %get-tuple-element.210, f32[256]{0:T(256)S(1)} %get-tuple-element.209), channel_id=1, replica_groups=mesh['var'=32,'samp'=8] {'samp'}, use_global_device_ids=true, to_apply=%region_4.5 | all-reduce | flops 512 | bytes 4096 | tf_op jit(solution)/shard_map/psum | solution.py:34
  40.0 2.7 scatter-add.56
  53.8 2.0 fusion.18
  57.2 2.0 fusion.19
  61.4 2.0 fusion.20
  63.4 13.8 %collective-permute-done.3 = f32[512,256]{1,0:T(8,128)} collective-permute-done((f32[512,256]{1,0:T(8,128)S(1)}, f32[512,256]{1,0:T(8,128)}, u32[]{:S(2)}, u32[]{:S(2)}) %collective-permute-start.3) | collective-permute-done | bytes 524320 | tf_op jit(solution)/shard_map/ppermute | solution.py:12
  78.5 2.0 fusion.21
  81.8 2.8 fusion.22
  90.6 79.0 %collective-permute-done.7 = f32[512,256]{1,0:T(8,128)S(1)} collective-permute-done((f32[512,256]{1,0:T(8,128)S(1)}, f32[512,256]{1,0:T(8,128)S(1)}, u32[]{:S(2)}, u32[]{:S(2)}) %collective-permute-start.7) | collective-permute-done | bytes 524320 | tf_op jit(solution)/shard_map/ppermute | solution.py:12
  169.6 12.0 %collective-permute-start.12 = (f32[512,256]{1,0:T(8,128)S(1)}, f32[512,256]{1,0:T(8,128)S(1)}, u32[]{:S(2)}, u32[]{:S(2)}) collective-permute-start(f32[512,256]{1,0:T(8,128)S(1)} %subtract_multiply_fusion), channel_id=1, source_target_pairs={{104,0},{112,8},{120,16},{128,24},{136,32},{144,40},{152,48},{160,... | collective-permute-start | bytes 1572872 | tf_op jit(solution)/shard_map/ppermute | solution.py:12
  192.4 72.9 %collective-permute-done.11 = f32[512,256]{1,0:T(8,128)S(1)} collective-permute-done((f32[512,256]{1,0:T(8,128)S(1)}, f32[512,256]{1,0:T(8,128)S(1)}, u32[]{:S(2)}, u32[]{:S(2)}) %collective-permute-start.11) | collective-permute-done | bytes 524320 | tf_op jit(solution)/shard_map/ppermute | solution.py:12
  294.0 2.0 fusion.31
  297.9 2.0 fusion.32
  301.9 2.0 fusion.33
  304.9 2.9 fusion
  307.8 2.9 fusion.1
  310.7 2.9 fusion.2
  313.7 3.0 fusion.3
  316.7 3.0 fusion.4
  319.6 2.8 fusion.5
  322.5 2.7 fusion.6
  325.2 2.7 fusion.7
  327.9 2.8 fusion.8
  330.7 2.7 fusion.9
  333.4 2.8 fusion.10
  336.2 2.7 fusion.11
  338.9 2.6 fusion.12
  341.5 2.8 fusion.13
  344.3 2.6 fusion.14
  347.0 2.1 fusion.15
  349.0 4.7 slice.440
  353.7 175.9 %reduce-scatter.2.cloned.1.call-done = f32[256,512]{1,0:T(8,128)} async-done(((f32[256,4096]{1,0:T(8,128)}), f32[256,512]{1,0:T(8,128)}) %reduce-scatter.2.cloned.1.call-update) | async-done | bytes 524304 | tf_op jit(solution)/shard_map/reduce_scatter | solution.py:51
  (168 shorter events, 80.9 us)
Async XLA Ops:
  6.5 523.1 %reduce-scatter.2.cloned.1.call-start = ((), (), s32[]{:S(2)}) async-start(), calls=%async_computation.1 | async-start | bytes 4718592 | tf_op jit(solution)/shard_map/reduce_scatter | solution.py:51
  30.0 22.6 %collective-permute-start = (f32[512,256]{1,0:T(8,128)S(1)}, f32[512,256]{1,0:T(8,128)}, u32[]{:S(2)}, u32[]{:S(2)}) collective-permute-start(f32[512,256]{1,0:T(8,128)S(1)} %subtract_multiply_fusion), channel_id=1, source_target_pairs={{8,0},{16,8},{24,16},{32,24},{40,32},{48,40},{56,48},{64,56},{72,6... | collective-permute-start | bytes 1572872 | tf_op jit(solution)/shard_map/ppermute | solution.py:12
  31.3 24.6 %collective-permute-start.1 = (f32[512,256]{1,0:T(8,128)S(1)}, f32[512,256]{1,0:T(8,128)}, u32[]{:S(2)}, u32[]{:S(2)}) collective-permute-start(f32[512,256]{1,0:T(8,128)S(1)} %subtract_multiply_fusion), channel_id=1, source_target_pairs={{16,0},{24,8},{32,16},{40,24},{48,32},{56,40},{64,48},{72,56},{80,... | collective-permute-start | bytes 1572872 | tf_op jit(solution)/shard_map/ppermute | solution.py:12
  32.6 26.7 %collective-permute-start.2 = (f32[512,256]{1,0:T(8,128)S(1)}, f32[512,256]{1,0:T(8,128)S(1)}, u32[]{:S(2)}, u32[]{:S(2)}) collective-permute-start(f32[512,256]{1,0:T(8,128)S(1)} %subtract_multiply_fusion), channel_id=1, source_target_pairs={{24,0},{32,8},{40,16},{48,24},{56,32},{64,40},{72,48},{80,56},{88,... | collective-permute-start | bytes 1572872 | tf_op jit(solution)/shard_map/ppermute | solution.py:12
  33.9 43.3 %collective-permute-start.3 = (f32[512,256]{1,0:T(8,128)S(1)}, f32[512,256]{1,0:T(8,128)}, u32[]{:S(2)}, u32[]{:S(2)}) collective-permute-start(f32[512,256]{1,0:T(8,128)S(1)} %subtract_multiply_fusion), channel_id=1, source_target_pairs={{32,0},{40,8},{48,16},{56,24},{64,32},{72,40},{80,48},{88,56},{96,... | collective-permute-start | bytes 1572872 | tf_op jit(solution)/shard_map/ppermute | solution.py:12
  35.2 45.3 %collective-permute-start.4 = (f32[512,256]{1,0:T(8,128)S(1)}, f32[512,256]{1,0:T(8,128)}, u32[]{:S(2)}, u32[]{:S(2)}) collective-permute-start(f32[512,256]{1,0:T(8,128)S(1)} %subtract_multiply_fusion), channel_id=1, source_target_pairs={{40,0},{48,8},{56,16},{64,24},{72,32},{80,40},{88,48},{96,56},{104... | collective-permute-start | bytes 1572872 | tf_op jit(solution)/shard_map/ppermute | solution.py:12
  52.6 32.0 %collective-permute-start.5 = (f32[512,256]{1,0:T(8,128)S(1)}, f32[512,256]{1,0:T(8,128)S(1)}, u32[]{:S(2)}, u32[]{:S(2)}) collective-permute-start(f32[512,256]{1,0:T(8,128)S(1)} %subtract_multiply_fusion), channel_id=1, source_target_pairs={{48,0},{56,8},{64,16},{72,24},{80,32},{88,40},{96,48},{104,56},{11... | collective-permute-start | bytes 1572872 | tf_op jit(solution)/shard_map/ppermute | solution.py:12
  55.9 31.7 %collective-permute-start.6 = (f32[512,256]{1,0:T(8,128)S(1)}, f32[512,256]{1,0:T(8,128)S(1)}, u32[]{:S(2)}, u32[]{:S(2)}) collective-permute-start(f32[512,256]{1,0:T(8,128)S(1)} %subtract_multiply_fusion), channel_id=1, source_target_pairs={{56,0},{64,8},{72,16},{80,24},{88,32},{96,40},{104,48},{112,56},{1... | collective-permute-start | bytes 1572872 | tf_op jit(solution)/shard_map/ppermute | solution.py:12
  60.1 109.6 %collective-permute-start.7 = (f32[512,256]{1,0:T(8,128)S(1)}, f32[512,256]{1,0:T(8,128)S(1)}, u32[]{:S(2)}, u32[]{:S(2)}) collective-permute-start(f32[512,256]{1,0:T(8,128)S(1)} %subtract_multiply_fusion), channel_id=1, source_target_pairs={{64,0},{72,8},{80,16},{88,24},{96,32},{104,40},{112,48},{120,56},{... | collective-permute-start | bytes 1572872 | tf_op jit(solution)/shard_map/ppermute | solution.py:12
  77.2 106.2 %collective-permute-start.8 = (f32[512,256]{1,0:T(8,128)S(1)}, f32[512,256]{1,0:T(8,128)S(1)}, u32[]{:S(2)}, u32[]{:S(2)}) collective-permute-start(f32[512,256]{1,0:T(8,128)S(1)} %subtract_multiply_fusion), channel_id=1, source_target_pairs={{72,0},{80,8},{88,16},{96,24},{104,32},{112,40},{120,48},{128,56},... | collective-permute-start | bytes 1572872 | tf_op jit(solution)/shard_map/ppermute | solution.py:12
  80.5 105.8 %collective-permute-start.9 = (f32[512,256]{1,0:T(8,128)S(1)}, f32[512,256]{1,0:T(8,128)S(1)}, u32[]{:S(2)}, u32[]{:S(2)}) collective-permute-start(f32[512,256]{1,0:T(8,128)S(1)} %subtract_multiply_fusion), channel_id=1, source_target_pairs={{80,0},{88,8},{96,16},{104,24},{112,32},{120,40},{128,48},{136,56}... | collective-permute-start | bytes 1572872 | tf_op jit(solution)/shard_map/ppermute | solution.py:12
  84.6 104.8 %collective-permute-start.10 = (f32[512,256]{1,0:T(8,128)S(1)}, f32[512,256]{1,0:T(8,128)S(1)}, u32[]{:S(2)}, u32[]{:S(2)}) collective-permute-start(f32[512,256]{1,0:T(8,128)S(1)} %subtract_multiply_fusion), channel_id=1, source_target_pairs={{88,0},{96,8},{104,16},{112,24},{120,32},{128,40},{136,48},{144,56... | collective-permute-start | bytes 1572872 | tf_op jit(solution)/shard_map/ppermute | solution.py:12
  87.6 177.7 %collective-permute-start.11 = (f32[512,256]{1,0:T(8,128)S(1)}, f32[512,256]{1,0:T(8,128)S(1)}, u32[]{:S(2)}, u32[]{:S(2)}) collective-permute-start(f32[512,256]{1,0:T(8,128)S(1)} %subtract_multiply_fusion), channel_id=1, source_target_pairs={{96,0},{104,8},{112,16},{120,24},{128,32},{136,40},{144,48},{152,5... | collective-permute-start | bytes 1572872 | tf_op jit(solution)/shard_map/ppermute | solution.py:12
  169.6 97.7 %collective-permute-start.12 = (f32[512,256]{1,0:T(8,128)S(1)}, f32[512,256]{1,0:T(8,128)S(1)}, u32[]{:S(2)}, u32[]{:S(2)}) collective-permute-start(f32[512,256]{1,0:T(8,128)S(1)} %subtract_multiply_fusion), channel_id=1, source_target_pairs={{104,0},{112,8},{120,16},{128,24},{136,32},{144,40},{152,48},{160,... | collective-permute-start | bytes 1572872 | tf_op jit(solution)/shard_map/ppermute | solution.py:12
  183.4 110.6 %collective-permute-start.13 = (f32[512,256]{1,0:T(8,128)S(1)}, f32[512,256]{1,0:T(8,128)}, u32[]{:S(2)}, u32[]{:S(2)}) collective-permute-start(f32[512,256]{1,0:T(8,128)S(1)} %subtract_multiply_fusion), channel_id=1, source_target_pairs={{112,0},{120,8},{128,16},{136,24},{144,32},{152,40},{160,48},{168,... | collective-permute-start | bytes 1572872 | tf_op jit(solution)/shard_map/ppermute | solution.py:12
  186.4 111.5 %collective-permute-start.14 = (f32[512,256]{1,0:T(8,128)S(1)}, f32[512,256]{1,0:T(8,128)}, u32[]{:S(2)}, u32[]{:S(2)}) collective-permute-start(f32[512,256]{1,0:T(8,128)S(1)} %subtract_multiply_fusion), channel_id=1, source_target_pairs={{120,0},{128,8},{136,16},{144,24},{152,32},{160,40},{168,48},{176,... | collective-permute-start | bytes 1572872 | tf_op jit(solution)/shard_map/ppermute | solution.py:12
  189.4 112.5 %collective-permute-start.15 = (f32[512,256]{1,0:T(8,128)S(1)}, f32[512,256]{1,0:T(8,128)}, u32[]{:S(2)}, u32[]{:S(2)}) collective-permute-start(f32[512,256]{1,0:T(8,128)S(1)} %subtract_multiply_fusion), channel_id=1, source_target_pairs={{128,0},{136,8},{144,16},{152,24},{160,32},{168,40},{176,48},{184,... | collective-permute-start | bytes 1572872 | tf_op jit(solution)/shard_map/ppermute | solution.py:12
  274.8 3.7 copy-start.12
  276.7 3.8 copy-start.13
  284.4 3.9 copy-start.18
  286.3 3.9 copy-start.15
  288.4 3.7 copy-start.11
  304.9 14.8 %copy-start = (f32[256,769]{1,0:T(8,128)S(1)}, f32[256,769]{1,0:T(8,128)}, u32[]{:S(2)}) copy-start(f32[256,769]{1,0:T(8,128)} %reshape.511) | copy-start | bytes 2362372
  304.9 17.6 %copy-start.1 = (f32[256,769]{1,0:T(8,128)S(1)}, f32[256,769]{1,0:T(8,128)}, u32[]{:S(2)}) copy-start(f32[256,769]{1,0:T(8,128)} %reshape.513) | copy-start | bytes 2362372
  307.8 17.4 %copy-start.2 = (f32[256,769]{1,0:T(8,128)S(1)}, f32[256,769]{1,0:T(8,128)}, u32[]{:S(2)}) copy-start(f32[256,769]{1,0:T(8,128)} %reshape.515) | copy-start | bytes 2362372
  310.7 17.2 %copy-start.3 = (f32[256,769]{1,0:T(8,128)S(1)}, f32[256,769]{1,0:T(8,128)}, u32[]{:S(2)}) copy-start(f32[256,769]{1,0:T(8,128)} %reshape.517) | copy-start | bytes 2362372
  313.7 17.0 %copy-start.4 = (f32[256,769]{1,0:T(8,128)S(1)}, f32[256,769]{1,0:T(8,128)}, u32[]{:S(2)}) copy-start(f32[256,769]{1,0:T(8,128)} %reshape.519) | copy-start | bytes 2362372
  316.7 16.7 %copy-start.5 = (f32[256,769]{1,0:T(8,128)S(1)}, f32[256,769]{1,0:T(8,128)}, u32[]{:S(2)}) copy-start(f32[256,769]{1,0:T(8,128)} %reshape.521) | copy-start | bytes 2362372
  319.6 16.5 %copy-start.6 = (f32[256,769]{1,0:T(8,128)S(1)}, f32[256,769]{1,0:T(8,128)}, u32[]{:S(2)}) copy-start(f32[256,769]{1,0:T(8,128)} %reshape.523) | copy-start | bytes 2362372
  322.5 16.4 %copy-start.7 = (f32[256,769]{1,0:T(8,128)S(1)}, f32[256,769]{1,0:T(8,128)}, u32[]{:S(2)}) copy-start(f32[256,769]{1,0:T(8,128)} %reshape.525) | copy-start | bytes 2362372
  325.2 16.3 %copy-start.8 = (f32[256,769]{1,0:T(8,128)S(1)}, f32[256,769]{1,0:T(8,128)}, u32[]{:S(2)}) copy-start(f32[256,769]{1,0:T(8,128)} %reshape.527) | copy-start | bytes 2362372
  327.9 16.4 %copy-start.9 = (f32[256,769]{1,0:T(8,128)S(1)}, f32[256,769]{1,0:T(8,128)}, u32[]{:S(2)}) copy-start(f32[256,769]{1,0:T(8,128)} %reshape.529) | copy-start | bytes 2362372
  (5 other events, 15.5 us)
Sparse Core Ops, SparseCore 0:
  353.8 175.7 reduce-scatter.1
where the time goes:
time: 549 us; the launch traced here: 539 us
  waiting for transfers between devices  342 us (62%)
  other arithmetic  59.6 us (11%)
  local copies, waits for them, and re-layouts  38.3 us (7%)
  matrix products  31.8 us (6%)
  starting transfers between devices  31.3 us (6%)
  blocking collectives  21.2 us (4%)
  between operations  14.5 us (3%)
    reduce_scatter x1, waiting for transfers between devices, body(): lax.psum_scatter(band_part, 'samp', scatter_dimension=1, tiled=True)  176 us
    ppermute x16, waiting for transfers between devices, shifted(): return lax.ppermute(block, axis, route)  166 us
    scatter-add x16, other arithmetic, body(): holder.at[:, first:first + 2 * block_width]  44.1 us
    dot_general x17, matrix products, gram_tile(): lax.dot_general(left, right, (((0,), (0,)), ((), ())), precision=lax.Prec...  31.8 us
    ppermute x16, starting transfers between devices, shifted(): return lax.ppermute(block, axis, route)  31.3 us
    reshape x17, local copies, waits for them, and re-layouts, skew_tile(): return flattened.reshape(width, 3 * width + 1)[:, 1:1 + 2 * width]  27.3 us
    psum x1, blocking collectives, body(): lax.psum((jnp.sum(dosage, axis=0), jnp.sum(dosage * dosage, axis=0)), 'sa...  21.2 us
    another operation x17, other arithmetic  11.4 us
  transfers between devices with their start and end apart: 17, of which 5 were waited for; matrix products, arithmetic and copies ran while one was open for 14% of the time, Pallas kernels for 0%

commit v1 on v0

v1 whole, which is shorter than its diff:
```python
import jax
import jax.numpy as jnp
from jax import lax
from jax.experimental import pallas as pl
from jax.experimental.pallas import tpu as pltpu
from jax.sharding import PartitionSpec as P

MESH = pl.DeviceIdType.MESH
SAMPLES = 4096
VARIANTS = 8192
W = 256
K = 512
L = 128
NZ, NX = 8, 4
F32, BF16 = jnp.float32, jnp.bfloat16


def split(a):
    hi = a.astype(BF16)
    return hi, (a - hi.astype(F32)).astype(BF16)


def kernel(
    x_ref, o_ref,
    stat_out, stat_in, cols, rows_in, lhs, gram, part, half_in, full_in, y_in,
    stat_ss, stat_rs, row_ss, row_rs, z_ss, z_rs, sib_ss, sib_rs, x_ss, h_rs, f_rs, y_ss, y_rs,
):
    v, samp = lax.axis_index("var"), lax.axis_index("samp")
    z, yl, c = v // 4, (v // 2) % 2, v % 2
    yh, x = samp // 4, samp % 4

    def device(z=z, yl=yl, c=c, yh=yh, x=x):
        return (z * 4 + yl * 2 + c, yh * 4 + x)

    def remote(src, dst, ss, rs, to):
        return pltpu.make_async_remote_copy(
            src_ref=src, dst_ref=dst, send_sem=ss, recv_sem=rs, device_id=to, device_id_type=MESH
        )

    z_up, z_down = (z + 1) % NZ, (z + NZ - 1) % NZ
    x_right, x_left = (x + 1) % NX, (x + NX - 1) % NX
    sibling = device(c=1 - c)
    peers = [device(yh=(yh + k // 4) % 2, x=(x + k % 4) % NX) for k in range(1, 8)]
    others = [sibling, device(yl=1 - yl), device(yl=1 - yl, yh=1 - yh), device(z=z_up), device(z=z_down)]

    barrier = pltpu.get_barrier_semaphore()
    for to in peers + others:
        pl.semaphore_signal(barrier, inc=1, device_id=to, device_id_type=MESH)

    dose = x_ref[...]
    total = jnp.sum(dose, axis=0, keepdims=True)
    square = jnp.sum(dose * dose, axis=0, keepdims=True)
    line = lax.broadcasted_iota(jnp.int32, (8, W), 0)
    stat_out[...] = jnp.where(line == 0, total, jnp.where(line == 1, square, 0.0))
    pl.semaphore_wait(barrier, len(peers) + len(others))
    stat_copies = [
        remote(stat_out, stat_in.at[k - 1], stat_ss.at[k - 1], stat_rs.at[k - 1], peers[k - 1])
        for k in range(1, 8)
    ]
    for copy in stat_copies:
        copy.start()
    for copy in stat_copies:
        copy.wait_recv()
    sums = stat_out[...]
    for k in range(7):
        sums = sums + stat_in[k]
    mean = sums[0:1] / SAMPLES
    inv = lax.rsqrt(sums[1:2] / SAMPLES - mean * mean + 1e-06)
    standard = (dose - mean) * inv
    for h in range(2):
        cols[0, c, h] = standard[:, h * L : (h + 1) * L]

    def z_copy(dist, h):
        return remote(
            cols.at[dist, c, h], cols.at[dist + 1, c, h], z_ss.at[dist, h], z_rs.at[dist, h], device(z=z_down)
        )

    def sib_copy(dist, h):
        return remote(cols.at[dist, c, h], cols.at[dist, c, h], sib_ss.at[dist, h], sib_rs.at[dist, h], sibling)

    row_copy = remote(cols.at[0, c], rows_in, row_ss, row_rs, device(yl=1 - yl))
    z_copy(0, 0).start()
    row_copy.start()
    z_copy(0, 1).start()
    for h in range(2):
        sib_copy(0, h).start()

    def put_rows(index, first, block):
        hi, lo = split(block)
        spot = (index, pl.ds(first, block.shape[0]))
        lhs[spot + (pl.ds(0, K),)] = hi
        lhs[spot + (pl.ds(K, K),)] = lo
        lhs[spot + (pl.ds(2 * K, K),)] = hi

    put_rows(yl, 0, standard.T)

    def multiply(dist, h):
        right = jnp.concatenate([cols[dist, 0, h], cols[dist, 1, h]], axis=1)
        hi, lo = split(right)
        right = jnp.concatenate([hi, hi, lo], axis=0)
        for r in range(2):
            out = jnp.dot(lhs[r], right, preferred_element_type=F32)
            gram[h, dist, r, 0] = out[:, :L]
            gram[h, dist, r, 1] = out[:, L:]

    row_id = lax.broadcasted_iota(jnp.int32, (W, L), 0)
    lane_id = lax.broadcasted_iota(jnp.int32, (W, L), 1)

    def tile(h, d):
        c2 = (c + d) % 2
        dist = (d - 2 * yl + c + 2) // 4
        r = (yl + 8 * 2 - (d - (c2 - c)) // 2) % 2
        return gram[h, dist, r, c2]

    def build(h, s):
        first = jnp.where(lane_id + h * L > row_id, tile(h, 2 * s), tile(h, 2 * s + 2))
        second = tile(h, 2 * s + 1)
        for p in range(2):
            part[h, s, 0, p] = first[p * L : (p + 1) * L]
            part[h, s, 1, p] = second[p * L : (p + 1) * L]

    def role(s):
        return (s % 4 + NX - x) % NX

    def side(s):
        return (role(s) - 1) // 2

    def far_copy(h, s, p):
        to = device(x=x_right if p == 0 else x_left)
        return remote(part.at[h, s, :, p], half_in.at[h, s], x_ss.at[h, s, p], h_rs.at[h, s], to)

    def near_copy(h, s, p):
        q = side(s)
        to = device(x=(x + 1 + 2 * q) % NX)
        return remote(
            part.at[h, s, :, p], full_in.at[h, s // 4, q, :, p], x_ss.at[h, s, p], f_rs.at[h, s // 4, q, p], to
        )

    def send_first(h, s):
        @pl.when(role(s) == 2)
        def _():
            far_copy(h, s, 0).start()
            far_copy(h, s, 1).start()

        @pl.when(role(s) % 2 == 1)
        def _():
            near_copy(h, s, 1 - side(s)).start()

    def send_second(h, s):
        @pl.when(role(s) % 2 == 1)
        def _():
            p = side(s)
            far_copy(h, s, 0).wait_recv()
            part[h, s, :, p] = part[h, s, :, p] + half_in[h, s]
            near_copy(h, s, p).start()

    def y_copy(h, s, yl2, t):
        me = 2 * yh + yl
        return remote(
            part.at[h, s, t], y_in.at[h, me, t], y_ss.at[h, s // 4, yl2, t], y_rs.at[h, me, t],
            device(yh=s // 4, yl=yl2),
        )

    def to_y(h, s, act):
        for yl2 in range(2):
            away = jnp.logical_or(s // 4 != yh, yl2 != yl)
            wanted = (yl + yl2 + s) % 2 == c

            @pl.when(away)
            def _():
                act(y_copy(h, s, yl2, 0))

            @pl.when(jnp.logical_and(away, wanted))
            def _():
                act(y_copy(h, s, yl2, 1))

    def collect(h, s):
        @pl.when(role(s) == 0)
        def _():
            own = part[h, s]
            for q in range(2):
                for p in range(2):
                    remote(
                        part.at[h, s, :, p], full_in.at[h, s // 4, q, :, p], x_ss.at[h, s, p],
                        f_rs.at[h, s // 4, q, p], device(x=x_right),
                    ).wait_recv()
                own = own + full_in[h, s // 4, q]
            part[h, s] = own
            to_y(h, s, lambda copy: copy.start())

            @pl.when(s // 4 == yh)
            def _():
                y_in[h, 2 * yh + yl] = own

    row_copy.wait_recv()
    for h in range(2):
        put_rows(1 - yl, h * L, rows_in[h].T)
    for h in range(2):
        sib_copy(0, h).wait_recv()
        multiply(0, h)

    steps = [(dist, h) for dist in range(1, 5) for h in range(2)]
    units = [[(h, 2 * dist - 2), (h, 2 * dist - 1)] for dist, h in steps]
    for n, (dist, h) in enumerate(steps):
        z_copy(dist - 1, h).wait_recv()
        if dist < 4:
            z_copy(dist, h).start()
        sib_copy(dist, h).start()
        sib_copy(dist, h).wait_recv()
        multiply(dist, h)
        for unit in units[n]:
            build(*unit)
            send_first(*unit)
        if n >= 1:
            for unit in units[n - 1]:
                send_second(*unit)
        if n >= 2:
            for unit in units[n - 2]:
                collect(*unit)
    for unit in units[-1]:
        send_second(*unit)
    for unit in units[-2] + units[-1]:
        collect(*unit)

    me = 2 * yh + yl
    first_yl = (yl + x) % 2
    mid_yl = (yl + x + c) % 2
    pieces = [[None, None], [None, None]]
    for h in range(2):
        for src in range(4):
            @pl.when(me != src)
            def _():
                remote(part.at[h, 0, 0], y_in.at[h, src, 0], y_ss.at[h, 0, 0, 0], y_rs.at[h, src, 0], sibling).wait_recv()

                @pl.when((src % 2 + yl + x) % 2 == c)
                def _():
                    remote(
                        part.at[h, 0, 1], y_in.at[h, src, 1], y_ss.at[h, 0, 0, 1], y_rs.at[h, src, 1], sibling
                    ).wait_recv()

        upper = (y_in[h, first_yl, 0] + y_in[h, 2 + first_yl, 0]).reshape(W, L)
        lower = (y_in[h, 1 - first_yl, 0] + y_in[h, 3 - first_yl, 0]).reshape(W, L)
        pieces[0][h] = jnp.where(lane_id + h * L > row_id, upper, lower)
        pieces[1][h] = (y_in[h, mid_yl, 1] + y_in[h, 2 + mid_yl, 1]).reshape(W, L)
    band = jnp.concatenate(pieces[0] + pieces[1], axis=1) * (1.0 / 64.0)
    row = lax.broadcasted_iota(jnp.int32, (W, 2 * W), 0)
    shift = row + 1
    for bit in range(9):
        moved = pltpu.roll(band, 2 * W - 2**bit, 1)
        band = jnp.where((shift // 2**bit) % 2 == 1, moved, band)
    reach = v * W + row + 1 + samp * 2 * W + lax.broadcasted_iota(jnp.int32, (W, 2 * W), 1)
    o_ref[...] = jnp.where(reach < VARIANTS, band, 0.0)

    for copy in stat_copies:
        copy.wait_send()
    row_copy.wait_send()
    for h in range(2):
        for dist in range(5):
            if dist < 4:
                z_copy(dist, h).wait_send()
            sib_copy(dist, h).wait_send()
        for s in range(8):
            @pl.when(role(s) != 0)
            def _():
                for p in range(2):
                    far_copy(h, s, p).wait_send()

            @pl.when(role(s) == 0)
            def _():
                to_y(h, s, lambda copy: copy.wait_send())


def body(dosage):
    dma = pltpu.SemaphoreType.DMA
    return pl.pallas_call(
        kernel,
        out_shape=jax.ShapeDtypeStruct((W, 2 * W), F32),
        in_specs=[pl.BlockSpec(memory_space=pltpu.VMEM)],
        out_specs=pl.BlockSpec(memory_space=pltpu.VMEM),
        scratch_shapes=[
            pltpu.VMEM((8, W), F32),
            pltpu.VMEM((7, 8, W), F32),
            pltpu.VMEM((5, 2, 2, K, L), F32),
            pltpu.VMEM((2, K, L), F32),
            pltpu.VMEM((2, W, 3 * K), BF16),
            pltpu.VMEM((2, 5, 2, 2, W, L), F32),
            pltpu.VMEM((2, 8, 2, 2, L, L), F32),
            pltpu.VMEM((2, 8, 2, L, L), F32),
            pltpu.VMEM((2, 2, 2, 2, 2, L, L), F32),
            pltpu.VMEM((2, 4, 2, 2, L, L), F32),
            dma((7,)), dma((7,)),
            dma, dma,
            dma((4, 2)), dma((4, 2)),
            dma((5, 2)), dma((5, 2)),
            dma((2, 8, 2)), dma((2, 8)), dma((2, 2, 2, 2)),
            dma((2, 2, 2, 2)), dma((2, 4, 2)),
        ],
        compiler_params=pltpu.CompilerParams(
            collective_id=0, has_side_effects=True, vmem_limit_bytes=48 * 2**20
        ),
        cost_estimate=pl.CostEstimate(flops=2 * 17 * W * W * K * 3, bytes_accessed=2**20, transcendentals=W),
    )(dosage)


def solution(mesh):
    return jax.shard_map(
        body, mesh=mesh, in_specs=(P("samp", "var"),), out_specs=P("var", "samp"), check_vma=False
    )
```

time: 549 us -> 102 us (0.19)
  the two profiles are of different devices: /device:TPU:2 before, /device:TPU:30 now
where the time goes in v1:
time: 102 us
  Pallas kernels  100 us (98%)
  local copies, waits for them, and re-layouts  1.84 us (2%)
    pallas_call x1, Pallas kernels, body(): pl.pallas_call(kernel, out_shape=jax.ShapeDtypeStruct((W, 2 * W), F32), i...  100 us

profile of v1, /device:TPU:30, one launch (start us, length us, event | category | flops | bytes accessed | tf_op | source)
XLA Modules:
  0.0 102.0 jit_solution(8191028879059860366)
XLA Ops:
  0.0 0.0 copy-start
  0.0 1.0 %copy-done = f32[512,256]{1,0:T(8,128)S(1)} copy-done((f32[512,256]{1,0:T(8,128)S(1)}, f32[512,256]{1,0:T(8,128)}, u32[]{:S(2)}) %copy-start) | copy-done | bytes 524312
  1.0 100.2 %shard_map.17 = f32[256,512]{1,0:T(8,128)S(1)} custom-call(f32[512,256]{1,0:T(8,128)S(1)} %copy-done), custom_call_target="tpu_custom_call" | custom-call | flops 3422552064 | bytes 1048576 | tf_op jit(solution)/shard_map/pallas_call | solution.py:275
  101.2 0.8 copy.3
Async XLA Ops:
  0.0 1.0 %copy-start = (f32[512,256]{1,0:T(8,128)S(1)}, f32[512,256]{1,0:T(8,128)}, u32[]{:S(2)}) copy-start(f32[512,256]{1,0:T(8,128)} %x_ref.1) | copy-start | bytes 1572868

commit v2 on v1

--- a/solution.py
+++ b/solution.py
@@ -12,6 +12,8 @@
 K = 512
 L = 128
 NZ, NX = 8, 4
+NP = 2
+KP = K // NP
 F32, BF16 = jnp.float32, jnp.bfloat16
 
 
@@ -22,8 +24,9 @@
 
 def kernel(
     x_ref, o_ref,
-    stat_out, stat_in, cols, rows_in, lhs, gram, part, half_in, full_in, y_in,
-    stat_ss, stat_rs, row_ss, row_rs, z_ss, z_rs, sib_ss, sib_rs, x_ss, h_rs, f_rs, y_ss, y_rs,
+    stat_out, stat_in, stat, row_stat, cols, rows_in, relay, lhs, gram, part, half_in, full_in, y_in,
+    stat_ss, stat_rs, zt_ss, zt_rs, st_ss, st_rs, rt_ss, rt_rs,
+    row_ss, row_rs, z_ss, z_rs, far_ss, far_rs, sib_ss, sib_rs, x_ss, h_rs, f_rs, y_ss, y_rs,
 ):
     v, samp = lax.axis_index("var"), lax.axis_index("samp")
     z, yl, c = v // 4, (v // 2) % 2, v % 2
@@ -42,23 +45,68 @@
     sibling = device(c=1 - c)
     peers = [device(yh=(yh + k // 4) % 2, x=(x + k % 4) % NX) for k in range(1, 8)]
     others = [sibling, device(yl=1 - yl), device(yl=1 - yl, yh=1 - yh), device(z=z_up), device(z=z_down)]
+    others += [device(z=(z + 2) % NZ), device(z=(z + 6) % NZ)]
 
     barrier = pltpu.get_barrier_semaphore()
     for to in peers + others:
         pl.semaphore_signal(barrier, inc=1, device_id=to, device_id_type=MESH)
+
+    def raw(h, first=0, count=K):
+        return x_ref.at[pl.ds(first, count), pl.ds(h * L, L)]
+
+    def z_copy(dist, h, p):
+        here = pl.ds(p * KP, KP)
+        src = cols.at[dist, c, h, here] if dist else raw(h, p * KP, KP)
+        return remote(
+            src, cols.at[dist + 1, c, h, here], z_ss.at[dist, h, p], z_rs.at[dist, h, p], device(z=z_down)
+        )
+
+    def far_copy(hop, h, p):
+        here = pl.ds(p * KP, KP)
+        src = relay.at[h, here] if hop else raw(h, p * KP, KP)
+        dst = cols.at[4, c, h, here] if hop else relay.at[h, here]
+        return remote(src, dst, far_ss.at[hop, h, p], far_rs.at[hop, h, p], device(z=(z + 2) % NZ))
+
+    def sib_copy(dist, h):
+        there = cols.at[dist, c, h]
+        return remote(there if dist else raw(h), there, sib_ss.at[dist, h], sib_rs.at[dist, h], sibling)
+
+    def row_copy(h):
+        return remote(raw(h), rows_in.at[h], row_ss.at[h], row_rs.at[h], device(yl=1 - yl))
+
+    def z_stat(dist):
+        return remote(
+            stat.at[dist, c], stat.at[dist + 1, c], zt_ss.at[dist], zt_rs.at[dist], device(z=z_down)
+        )
+
+    def sib_stat(dist):
+        return remote(stat.at[dist, c], stat.at[dist, c], st_ss.at[dist], st_rs.at[dist], sibling)
+
+    row_stat_copy = remote(stat.at[0, c], row_stat, rt_ss, rt_rs, device(yl=1 - yl))
+
+    def by_far(h, p):
+        return h == 0 or p == 0
 
     dose = x_ref[...]
     total = jnp.sum(dose, axis=0, keepdims=True)
     square = jnp.sum(dose * dose, axis=0, keepdims=True)
     line = lax.broadcasted_iota(jnp.int32, (8, W), 0)
     stat_out[...] = jnp.where(line == 0, total, jnp.where(line == 1, square, 0.0))
-    pl.semaphore_wait(barrier, len(peers) + len(others))
     stat_copies = [
         remote(stat_out, stat_in.at[k - 1], stat_ss.at[k - 1], stat_rs.at[k - 1], peers[k - 1])
         for k in range(1, 8)
     ]
+    pl.semaphore_wait(barrier, len(peers) + len(others))
     for copy in stat_copies:
         copy.start()
+    row_copy(0).start()
+    for p in range(NP):
+        z_copy(0, 0, p).start()
+    for p in range(NP):
+        far_copy(0, 0, p).start()
+    for h in range(2):
+        sib_copy(0, h).start()
+        cols[0, c, h] = dose[:, h * L : (h + 1) * L]
     for copy in stat_copies:
         copy.wait_recv()
     sums = stat_out[...]
@@ -66,24 +114,15 @@
         sums = sums + stat_in[k]
     mean = sums[0:1] / SAMPLES
     inv = lax.rsqrt(sums[1:2] / SAMPLES - mean * mean + 1e-06)
-    standard = (dose - mean) * inv
-    for h in range(2):
-        cols[0, c, h] = standard[:, h * L : (h + 1) * L]
-
-    def z_copy(dist, h):
-        return remote(
-            cols.at[dist, c, h], cols.at[dist + 1, c, h], z_ss.at[dist, h], z_rs.at[dist, h], device(z=z_down)
-        )
-
-    def sib_copy(dist, h):
-        return remote(cols.at[dist, c, h], cols.at[dist, c, h], sib_ss.at[dist, h], sib_rs.at[dist, h], sibling)
-
-    row_copy = remote(cols.at[0, c], rows_in, row_ss, row_rs, device(yl=1 - yl))
-    z_copy(0, 0).start()
-    row_copy.start()
-    z_copy(0, 1).start()
-    for h in range(2):
-        sib_copy(0, h).start()
+    stat[0, c] = jnp.where(line == 0, mean, inv)
+    z_stat(0).start()
+    row_stat_copy.start()
+    sib_stat(0).start()
+    row_copy(1).start()
+    for p in range(NP):
+        z_copy(0, 1, p).start()
+        if by_far(1, p):
+            far_copy(0, 1, p).start()
 
     def put_rows(index, first, block):
         hi, lo = split(block)
@@ -92,10 +131,14 @@
         lhs[spot + (pl.ds(K, K),)] = lo
         lhs[spot + (pl.ds(2 * K, K),)] = hi
 
-    put_rows(yl, 0, standard.T)
+    put_rows(yl, 0, ((dose - mean) * inv).T)
 
     def multiply(dist, h):
-        right = jnp.concatenate([cols[dist, 0, h], cols[dist, 1, h]], axis=1)
+        right = []
+        for c2 in range(2):
+            of = stat[dist, c2, :, h * L : (h + 1) * L]
+            right.append((cols[dist, c2, h] - of[0:1]) * of[1:2])
+        right = jnp.concatenate(right, axis=1)
         hi, lo = split(right)
         right = jnp.concatenate([hi, hi, lo], axis=0)
         for r in range(2):
@@ -125,7 +168,7 @@
     def side(s):
         return (role(s) - 1) // 2
 
-    def far_copy(h, s, p):
+    def far_half(h, s, p):
         to = device(x=x_right if p == 0 else x_left)
         return remote(part.at[h, s, :, p], half_in.at[h, s], x_ss.at[h, s, p], h_rs.at[h, s], to)
 
@@ -136,21 +179,30 @@
             part.at[h, s, :, p], full_in.at[h, s // 4, q, :, p], x_ss.at[h, s, p], f_rs.at[h, s // 4, q, p], to
         )
 
-    def send_first(h, s):
-        @pl.when(role(s) == 2)
-        def _():
-            far_copy(h, s, 0).start()
-            far_copy(h, s, 1).start()
-
-        @pl.when(role(s) % 2 == 1)
-        def _():
-            near_copy(h, s, 1 - side(s)).start()
+    def send_first(group):
+        for h, s in group:
+            @pl.when(role(s) == 2)
+            def _():
+                build(h, s)
+                far_half(h, s, 0).start()
+                far_half(h, s, 1).start()
+
+        for h, s in group:
+            @pl.when(role(s) % 2 == 1)
+            def _():
+                build(h, s)
+                near_copy(h, s, 1 - side(s)).start()
+
+        for h, s in group:
+            @pl.when(role(s) == 0)
+            def _():
+                build(h, s)
 
     def send_second(h, s):
         @pl.when(role(s) % 2 == 1)
         def _():
             p = side(s)
-            far_copy(h, s, 0).wait_recv()
+            far_half(h, s, 0).wait_recv()
             part[h, s, :, p] = part[h, s, :, p] + half_in[h, s]
             near_copy(h, s, p).start()
 
@@ -192,35 +244,91 @@
             def _():
                 y_in[h, 2 * yh + yl] = own
 
-    row_copy.wait_recv()
-    for h in range(2):
-        put_rows(1 - yl, h * L, rows_in[h].T)
-    for h in range(2):
-        sib_copy(0, h).wait_recv()
-        multiply(0, h)
-
-    steps = [(dist, h) for dist in range(1, 5) for h in range(2)]
+    steps = [(1, 0), (1, 1), (2, 0), (2, 1), (3, 0), (4, 0), (3, 1), (4, 1)]
     units = [[(h, 2 * dist - 2), (h, 2 * dist - 1)] for dist, h in steps]
-    for n, (dist, h) in enumerate(steps):
-        z_copy(dist - 1, h).wait_recv()
-        if dist < 4:
-            z_copy(dist, h).start()
+
+    def receive(n):
+        dist, h = steps[n]
+        if h == 0:
+            z_stat(dist - 1).wait_recv()
+            if dist < 4:
+                z_stat(dist).start()
+            sib_stat(dist).start()
+        for p in range(NP):
+            if dist == 4 and by_far(h, p):
+                far_copy(1, h, p).wait_recv()
+            else:
+                z_copy(dist - 1, h, p).wait_recv()
+            if dist < 3 or (dist == 3 and not by_far(h, p)):
+                z_copy(dist, h, p).start()
         sib_copy(dist, h).start()
+
+    def pass_on(h):
+        for p in range(NP):
+            if by_far(h, p):
+                far_copy(0, h, p).wait_recv()
+                far_copy(1, h, p).start()
+
+    def work(n):
+        dist, h = steps[n]
+        if dist == 1:
+            if h == 0:
+                sib_stat(0).wait_recv()
+            sib_copy(0, h).wait_recv()
+            multiply(0, h)
+        if h == 0:
+            sib_stat(dist).wait_recv()
         sib_copy(dist, h).wait_recv()
         multiply(dist, h)
+        send_first(units[n])
+
+    def second(n):
         for unit in units[n]:
-            build(*unit)
-            send_first(*unit)
-        if n >= 1:
-            for unit in units[n - 1]:
-                send_second(*unit)
-        if n >= 2:
-            for unit in units[n - 2]:
-                collect(*unit)
-    for unit in units[-1]:
-        send_second(*unit)
-    for unit in units[-2] + units[-1]:
-        collect(*unit)
+            send_second(*unit)
+
+    def gather(n):
+        for unit in units[n]:
+            collect(*unit)
+
+    receive(0)
+    row_stat_copy.wait_recv()
+    for h in range(2):
+        row_copy(h).wait_recv()
+        of = row_stat[:, h * L : (h + 1) * L]
+        put_rows(1 - yl, h * L, ((rows_in[h] - of[0:1]) * of[1:2]).T)
+    receive(1)
+    work(0)
+    pass_on(0)
+    work(1)
+    receive(2)
+    second(0)
+    second(1)
+    work(2)
+    receive(3)
+    second(2)
+    work(3)
+    pass_on(1)
+    gather(0)
+    gather(1)
+    receive(4)
+    second(3)
+    work(4)
+    receive(5)
+    work(5)
+    gather(2)
+    receive(6)
+    second(4)
+    second(5)
+    work(6)
+    gather(3)
+    receive(7)
+    second(6)
+    work(7)
+    gather(4)
+    gather(5)
+    second(7)
+    gather(6)
+    gather(7)
 
     me = 2 * yh + yl
     first_yl = (yl + x) % 2
@@ -253,17 +361,28 @@
 
     for copy in stat_copies:
         copy.wait_send()
-    row_copy.wait_send()
+    row_stat_copy.wait_send()
+    for dist in range(5):
+        if dist < 4:
+            z_stat(dist).wait_send()
+        sib_stat(dist).wait_send()
     for h in range(2):
+        row_copy(h).wait_send()
+        for p in range(NP):
+            for dist in range(3):
+                z_copy(dist, h, p).wait_send()
+            if by_far(h, p):
+                far_copy(0, h, p).wait_send()
+                far_copy(1, h, p).wait_send()
+            else:
+                z_copy(3, h, p).wait_send()
         for dist in range(5):
-            if dist < 4:
-                z_copy(dist, h).wait_send()
             sib_copy(dist, h).wait_send()
         for s in range(8):
             @pl.when(role(s) != 0)
             def _():
                 for p in range(2):
-                    far_copy(h, s, p).wait_send()
+                    far_half(h, s, p).wait_send()
 
             @pl.when(role(s) == 0)
             def _():
@@ -280,7 +399,10 @@
         scratch_shapes=[
             pltpu.VMEM((8, W), F32),
             pltpu.VMEM((7, 8, W), F32),
+            pltpu.VMEM((5, 2, 8, W), F32),
+            pltpu.VMEM((8, W), F32),
             pltpu.VMEM((5, 2, 2, K, L), F32),
+            pltpu.VMEM((2, K, L), F32),
             pltpu.VMEM((2, K, L), F32),
             pltpu.VMEM((2, W, 3 * K), BF16),
             pltpu.VMEM((2, 5, 2, 2, W, L), F32),
@@ -289,8 +411,8 @@
             pltpu.VMEM((2, 2, 2, 2, 2, L, L), F32),
             pltpu.VMEM((2, 4, 2, 2, L, L), F32),
             dma((7,)), dma((7,)),
-            dma, dma,
-            dma((4, 2)), dma((4, 2)),
+            dma((4,)), dma((4,)), dma((5,)), dma((5,)), dma, dma,
+            dma((2,)), dma((2,)), dma((4, 2, NP)), dma((4, 2, NP)), dma((2, 2, NP)), dma((2, 2, NP)),
             dma((5, 2)), dma((5, 2)),
             dma((2, 8, 2)), dma((2, 8)), dma((2, 2, 2, 2)),
             dma((2, 2, 2, 2)), dma((2, 4, 2)),

time: 102 us -> 84.7 us (0.83)
  the two profiles are of different devices: /device:TPU:30 before, /device:TPU:29 now
where the time goes in v2:
time: 84.7 us; the launch traced here: 84.6 us
  Pallas kernels  82.7 us (98%)
  local copies, waits for them, and re-layouts  1.84 us (2%)
    pallas_call x1, Pallas kernels, body(): pl.pallas_call(kernel, out_shape=jax.ShapeDtypeStruct((W, 2 * W), F32), i...  82.7 us
    unnamed x3, local copies, waits for them, and re-layouts  1.84 us

profile of v2, /device:TPU:29, one launch (start us, length us, event | category | flops | bytes accessed | tf_op | source)
XLA Modules:
  0.0 84.6 jit_solution(17222203247987122304)
XLA Ops:
  0.0 0.0 copy-start
  0.0 1.0 %copy-done = f32[512,256]{1,0:T(8,128)S(1)} copy-done((f32[512,256]{1,0:T(8,128)S(1)}, f32[512,256]{1,0:T(8,128)}, u32[]{:S(2)}) %copy-start) | copy-done | bytes 524312
  1.0 82.7 %shard_map.17 = f32[256,512]{1,0:T(8,128)S(1)} custom-call(f32[512,256]{1,0:T(8,128)S(1)} %copy-done), custom_call_target="tpu_custom_call" | custom-call | flops 3422552064 | bytes 1048576 | tf_op jit(solution)/shard_map/pallas_call | solution.py:394
  83.8 0.8 copy.3
Async XLA Ops:
  0.0 1.0 %copy-start = (f32[512,256]{1,0:T(8,128)S(1)}, f32[512,256]{1,0:T(8,128)}, u32[]{:S(2)}) copy-start(f32[512,256]{1,0:T(8,128)} %x_ref.1) | copy-start | bytes 1572868

commit v3 on v2

v3 whole, which is shorter than its diff:
```python
import jax
import jax.numpy as jnp
from jax import lax
from jax.experimental import pallas as pl
from jax.experimental.pallas import tpu as pltpu
from jax.sharding import PartitionSpec as P

MESH = pl.DeviceIdType.MESH
SAMPLES = 4096
VARIANTS = 8192
W = 256
K = 512
L = 128
NZ, NX = 8, 4
NP = 2
KP = K // NP
F32, BF16 = jnp.float32, jnp.bfloat16
STEPS = ((1, 0), (2, 0), (3, 0), (1, 1), (4, 0), (2, 1), (3, 1), (4, 1))
ORDER = (
    "H", "Y0", "R0", "Y1", "M00", "M01", "R3", "M30", "P0", "F01", "R1", "M10", "O10", "O00", "F30", "F00",
    "F10", "M11", "S10", "P1", "O30", "M31", "O11", "O01", "O31", "R5", "S00", "M50", "F50", "O50", "F11",
    "M51", "S01", "O51", "R2", "R4", "M20", "F51", "S30", "M21", "O20", "G10", "M40", "G00", "S51", "F21",
    "O21", "F31", "M41", "O40", "F40", "R6", "O41", "M60", "S21", "F41", "R7", "F20", "G51", "S40", "M61",
    "M70", "O70", "O60", "S41", "G21", "S20", "F70", "F60", "S50", "G40", "S60", "M71", "G30", "F61", "O61",
    "O71", "G01", "G20", "S31", "G41", "S70", "G60", "S11", "G50", "F71", "S71", "S61", "G70", "G11", "G61",
    "G31", "G71",
)


def split(a):
    hi = a.astype(BF16)
    return hi, (a - hi.astype(F32)).astype(BF16)


def kernel(
    x_ref, o_ref,
    stat_out, stat_in, stat, row_stat, cols, rows_in, relay, lhs, gram, part, half_in, full_in, y_in,
    stat_ss, stat_rs, zt_ss, zt_rs, st_ss, st_rs, rt_ss, rt_rs,
    row_ss, row_rs, z_ss, z_rs, far_ss, far_rs, sib_ss, sib_rs, x_ss, h_rs, f_rs, y_ss, y_rs,
):
    v, samp = lax.axis_index("var"), lax.axis_index("samp")
    z, yl, c = v // 4, (v // 2) % 2, v % 2
    yh, x = samp // 4, samp % 4

    def device(z=z, yl=yl, c=c, yh=yh, x=x):
        return (z * 4 + yl * 2 + c, yh * 4 + x)

    def remote(src, dst, ss, rs, to):
        return pltpu.make_async_remote_copy(
            src_ref=src, dst_ref=dst, send_sem=ss, recv_sem=rs, device_id=to, device_id_type=MESH
        )

    z_up, z_down = (z + 1) % NZ, (z + NZ - 1) % NZ
    x_right, x_left = (x + 1) % NX, (x + NX - 1) % NX
    sibling = device(c=1 - c)
    peers = [device(yh=(yh + k // 4) % 2, x=(x + k % 4) % NX) for k in range(1, 8)]
    others = [sibling, device(yl=1 - yl), device(yl=1 - yl, yh=1 - yh), device(z=z_up), device(z=z_down)]
    others += [device(z=(z + 2) % NZ), device(z=(z + 6) % NZ)]

    barrier = pltpu.get_barrier_semaphore()
    for to in peers + others:
        pl.semaphore_signal(barrier, inc=1, device_id=to, device_id_type=MESH)

    def raw(h, first=0, count=K):
        return cols.at[0, c, h, pl.ds(first, count)]

    def z_copy(dist, h, p):
        here = pl.ds(p * KP, KP)
        src = cols.at[dist, c, h, here] if dist else raw(h, p * KP, KP)
        return remote(
            src, cols.at[dist + 1, c, h, here], z_ss.at[dist, h, p], z_rs.at[dist, h, p], device(z=z_down)
        )

    def far_copy(hop, h, p):
        here = pl.ds(p * KP, KP)
        src = relay.at[h, here] if hop else raw(h, p * KP, KP)
        dst = cols.at[4, c, h, here] if hop else relay.at[h, here]
        return remote(src, dst, far_ss.at[hop, h, p], far_rs.at[hop, h, p], device(z=(z + 2) % NZ))

    def sib_copy(dist, h):
        there = cols.at[dist, c, h]
        return remote(there if dist else raw(h), there, sib_ss.at[dist, h], sib_rs.at[dist, h], sibling)

    def row_copy(h):
        return remote(raw(h), rows_in.at[h], row_ss.at[h], row_rs.at[h], device(yl=1 - yl))

    def z_stat(dist):
        return remote(
            stat.at[dist, c], stat.at[dist + 1, c], zt_ss.at[dist], zt_rs.at[dist], device(z=z_down)
        )

    def sib_stat(dist):
        return remote(stat.at[dist, c], stat.at[dist, c], st_ss.at[dist], st_rs.at[dist], sibling)

    row_stat_copy = remote(stat.at[0, c], row_stat, rt_ss, rt_rs, device(yl=1 - yl))

    def by_far(h, p):
        return h == 0 or p == 0

    dose = x_ref[...]
    for h in range(2):
        cols[0, c, h] = dose[:, h * L : (h + 1) * L]
    total = jnp.sum(dose, axis=0, keepdims=True)
    square = jnp.sum(dose * dose, axis=0, keepdims=True)
    line = lax.broadcasted_iota(jnp.int32, (8, W), 0)
    stat_out[...] = jnp.where(line == 0, total, jnp.where(line == 1, square, 0.0))
    stat_copies = [
        remote(stat_out, stat_in.at[k - 1], stat_ss.at[k - 1], stat_rs.at[k - 1], peers[k - 1])
        for k in range(1, 8)
    ]
    pl.semaphore_wait(barrier, len(peers) + len(others))
    for copy in stat_copies:
        copy.start()
    row_copy(0).start()
    for p in range(NP):
        z_copy(0, 0, p).start()
    for p in range(NP):
        far_copy(0, 0, p).start()
    for h in range(2):
        sib_copy(0, h).start()
    for copy in stat_copies:
        copy.wait_recv()
    sums = stat_out[...]
    for k in range(7):
        sums = sums + stat_in[k]
    mean = sums[0:1] / SAMPLES
    inv = lax.rsqrt(sums[1:2] / SAMPLES - mean * mean + 1e-06)
    stat[0, c] = jnp.where(line == 0, mean, inv)
    z_stat(0).start()
    row_stat_copy.start()
    sib_stat(0).start()
    row_copy(1).start()

    def put_rows(index, first, block):
        hi, lo = split(block)
        spot = (index, pl.ds(first, block.shape[0]))
        lhs[spot + (pl.ds(0, K),)] = hi
        lhs[spot + (pl.ds(K, K),)] = lo
        lhs[spot + (pl.ds(2 * K, K),)] = hi

    put_rows(yl, 0, ((dose - mean) * inv).T)

    def multiply(dist, h, p):
        right = []
        for c2 in range(2):
            of = stat[dist, c2, :, h * L : (h + 1) * L]
            right.append((cols[dist, c2, h] - of[0:1]) * of[1:2])
        hi, lo = split(jnp.concatenate(right, axis=1))
        right = jnp.concatenate([hi, hi, lo], axis=0)
        rows = pl.ds(p * L, L)
        for r in range(2):
            out = jnp.dot(lhs[r, rows], right, preferred_element_type=F32)
            gram[h, dist, r, 0, rows] = out[:, :L]
            gram[h, dist, r, 1, rows] = out[:, L:]

    row_id = lax.broadcasted_iota(jnp.int32, (L, L), 0)
    lane_id = lax.broadcasted_iota(jnp.int32, (L, L), 1)

    def tile(h, d, p):
        c2 = (c + d) % 2
        dist = (d - 2 * yl + c + 2) // 4
        r = (yl + 8 * 2 - (d - (c2 - c)) // 2) % 2
        return gram[h, dist, r, c2, pl.ds(p * L, L)]

    def build(h, s, p):
        above = lane_id + h * L > row_id + p * L
        part[h, s, p, 0] = jnp.where(above, tile(h, 2 * s, p), tile(h, 2 * s + 2, p))
        part[h, s, p, 1] = tile(h, 2 * s + 1, p)

    def role(s):
        return (s % 4 + NX - x) % NX

    def side(s):
        return (role(s) - 1) // 2

    def far_half(h, s, p, t):
        to = device(x=x_right if t == 0 else x_left)
        return remote(part.at[h, s, p, t], half_in.at[h, s, p], x_ss.at[h, s, p, t], h_rs.at[h, s, p], to)

    def near_copy(h, s, p, t):
        q = side(s)
        to = device(x=(x + 1 + 2 * q) % NX)
        return remote(
            part.at[h, s, p, t], full_in.at[h, s // 4, q, p, t], x_ss.at[h, s, p, t], f_rs.at[h, s // 4, q, p, t], to
        )

    def send_opposite(h, s, p):
        @pl.when(role(s) == 2)
        def _():
            build(h, s, p)
            far_half(h, s, p, 0).start()
            far_half(h, s, p, 1).start()

    def send_free(h, s, p):
        @pl.when(role(s) % 2 == 1)
        def _():
            build(h, s, p)
            near_copy(h, s, p, 1 - side(s)).start()

    def send_second(h, s, p):
        @pl.when(role(s) % 2 == 1)
        def _():
            t = side(s)
            far_half(h, s, p, 0).wait_recv()
            part[h, s, p, t] = part[h, s, p, t] + half_in[h, s, p]
            near_copy(h, s, p, t).start()

    def y_copy(h, s, yl2, p, t):
        me = 2 * yh + yl
        return remote(
            part.at[h, s, p, t], y_in.at[h, me, p, t], y_ss.at[h, s // 4, yl2, p, t], y_rs.at[h, me, p, t],
            device(yh=s // 4, yl=yl2),
        )

    def to_y(h, s, p, act):
        for yl2 in range(2):
            away = jnp.logical_or(s // 4 != yh, yl2 != yl)
            wanted = (yl + yl2 + s) % 2 == c

            @pl.when(away)
            def _():
                act(y_copy(h, s, yl2, p, 0))

            @pl.when(jnp.logical_and(away, wanted))
            def _():
                act(y_copy(h, s, yl2, p, 1))

    def collect(h, s, p):
        @pl.when(role(s) == 0)
        def _():
            build(h, s, p)
            for t in range(2):
                for q in range(2):
                    remote(
                        part.at[h, s, p, t], full_in.at[h, s // 4, q, p, t], x_ss.at[h, s, p, t],
                        f_rs.at[h, s // 4, q, p, t], device(x=x_right),
                    ).wait_recv()
                part[h, s, p, t] = part[h, s, p, t] + full_in[h, s // 4, 0, p, t] + full_in[h, s // 4, 1, p, t]
            to_y(h, s, p, lambda copy: copy.start())

            @pl.when(s // 4 == yh)
            def _():
                y_in[h, 2 * yh + yl, p] = part[h, s, p]

    def start_half():
        for p in range(NP):
            z_copy(0, 1, p).start()
            if by_far(1, p):
                far_copy(0, 1, p).start()

    def other_rows(p):
        if p == 0:
            row_stat_copy.wait_recv()
        row_copy(p).wait_recv()
        of = row_stat[:, p * L : (p + 1) * L]
        put_rows(1 - yl, p * L, ((rows_in[p] - of[0:1]) * of[1:2]).T)

    def receive(n):
        dist, h = STEPS[n]
        if h == 0:
            z_stat(dist - 1).wait_recv()
            if dist < 4:
                z_stat(dist).start()
            sib_stat(dist).start()
        for p in range(NP):
            if dist == 4 and by_far(h, p):
                far_copy(1, h, p).wait_recv()
            else:
                z_copy(dist - 1, h, p).wait_recv()
            if dist < 3 or (dist == 3 and not by_far(h, p)):
                z_copy(dist, h, p).start()
        sib_copy(dist, h).start()

    def pass_on(h):
        for p in range(NP):
            if by_far(h, p):
                far_copy(0, h, p).wait_recv()
                far_copy(1, h, p).start()

    def work(n, p):
        dist, h = STEPS[n]
        if p == 0:
            if dist == 1:
                if h == 0:
                    sib_stat(0).wait_recv()
                sib_copy(0, h).wait_recv()
            if h == 0:
                sib_stat(dist).wait_recv()
            sib_copy(dist, h).wait_recv()
        if dist == 1:
            multiply(0, h, p)
        multiply(dist, h, p)

    parts = dict(H=start_half, R=receive, P=pass_on, Y=other_rows, M=work)
    each = dict(O=send_opposite, F=send_free, S=send_second, G=collect)
    for event in ORDER:
        kind, digits = event[0], [int(digit) for digit in event[1:]]
        if kind in parts:
            parts[kind](*digits)
        else:
            dist, h = STEPS[digits[0]]
            for unit in (2 * dist - 2, 2 * dist - 1):
                each[kind](h, unit, digits[1])

    me = 2 * yh + yl
    first_yl = (yl + x) % 2
    mid_yl = (yl + x + c) % 2

    def landed(h, src, p, t):
        return remote(
            part.at[h, 0, p, t], y_in.at[h, src, p, t], y_ss.at[h, 0, 0, p, t], y_rs.at[h, src, p, t], sibling
        )

    row = lax.broadcasted_iota(jnp.int32, (L, 2 * W), 0)
    lane = lax.broadcasted_iota(jnp.int32, (L, 2 * W), 1)
    for p in range(2):
        pieces = [[None, None], [None, None]]
        for h in range(2):
            for src in range(4):
                @pl.when(me != src)
                def _():
                    landed(h, src, p, 0).wait_recv()

                    @pl.when((src % 2 + yl + x) % 2 == c)
                    def _():
                        landed(h, src, p, 1).wait_recv()

            upper = y_in[h, first_yl, p, 0] + y_in[h, 2 + first_yl, p, 0]
            lower = y_in[h, 1 - first_yl, p, 0] + y_in[h, 3 - first_yl, p, 0]
            pieces[0][h] = jnp.where(lane_id + h * L > row_id + p * L, upper, lower)
            pieces[1][h] = y_in[h, mid_yl, p, 1] + y_in[h, 2 + mid_yl, p, 1]
        band = jnp.concatenate(pieces[0] + pieces[1], axis=1) * (1.0 / 64.0)
        shift = row + (p * L + 1)
        for bit in range(9):
            moved = pltpu.roll(band, 2 * W - 2**bit, 1)
            band = jnp.where((shift & 2**bit) != 0, moved, band)
        reach = v * W + shift + samp * 2 * W + lane
        o_ref[p * L : (p + 1) * L] = jnp.where(reach < VARIANTS, band, 0.0)

    for copy in stat_copies:
        copy.wait_send()
    row_stat_copy.wait_send()
    for dist in range(5):
        if dist < 4:
            z_stat(dist).wait_send()
        sib_stat(dist).wait_send()
    for h in range(2):
        row_copy(h).wait_send()
        for p in range(NP):
            for dist in range(3):
                z_copy(dist, h, p).wait_send()
            if by_far(h, p):
                far_copy(0, h, p).wait_send()
                far_copy(1, h, p).wait_send()
            else:
                z_copy(3, h, p).wait_send()
        for dist in range(5):
            sib_copy(dist, h).wait_send()
        for s in range(8):
            @pl.when(role(s) != 0)
            def _():
                for p in range(2):
                    for t in range(2):
                        far_half(h, s, p, t).wait_send()

            @pl.when(role(s) == 0)
            def _():
                for p in range(2):
                    to_y(h, s, p, lambda copy: copy.wait_send())


def body(dosage):
    dma = pltpu.SemaphoreType.DMA
    return pl.pallas_call(
        kernel,
        out_shape=jax.ShapeDtypeStruct((W, 2 * W), F32),
        in_specs=[pl.BlockSpec(memory_space=pltpu.VMEM)],
        out_specs=pl.BlockSpec(memory_space=pltpu.VMEM),
        scratch_shapes=[
            pltpu.VMEM((8, W), F32),
            pltpu.VMEM((7, 8, W), F32),
            pltpu.VMEM((5, 2, 8, W), F32),
            pltpu.VMEM((8, W), F32),
            pltpu.VMEM((5, 2, 2, K, L), F32),
            pltpu.VMEM((2, K, L), F32),
            pltpu.VMEM((2, K, L), F32),
            pltpu.VMEM((2, W, 3 * K), BF16),
            pltpu.VMEM((2, 5, 2, 2, W, L), F32),
            pltpu.VMEM((2, 8, 2, 2, L, L), F32),
            pltpu.VMEM((2, 8, 2, L, L), F32),
            pltpu.VMEM((2, 2, 2, 2, 2, L, L), F32),
            pltpu.VMEM((2, 4, 2, 2, L, L), F32),
            dma((7,)), dma((7,)),
            dma((4,)), dma((4,)), dma((5,)), dma((5,)), dma, dma,
            dma((2,)), dma((2,)), dma((4, 2, NP)), dma((4, 2, NP)), dma((2, 2, NP)), dma((2, 2, NP)),
            dma((5, 2)), dma((5, 2)),
            dma((2, 8, 2, 2)), dma((2, 8, 2)), dma((2, 2, 2, 2, 2)),
            dma((2, 2, 2, 2, 2)), dma((2, 4, 2, 2)),
        ],
        compiler_params=pltpu.CompilerParams(
            collective_id=0, has_side_effects=True, vmem_limit_bytes=48 * 2**20
        ),
        cost_estimate=pl.CostEstimate(flops=2 * 17 * W * W * K * 3, bytes_accessed=2**20, transcendentals=W),
    )(dosage)


def solution(mesh):
    return jax.shard_map(
        body, mesh=mesh, in_specs=(P("samp", "var"),), out_specs=P("var", "samp"), check_vma=False
    )
```

time: 84.7 us -> 80.1 us (0.946)
  the two profiles are of different devices: /device:TPU:29 before, /device:TPU:30 now
where the time goes in v3:
time: 80.1 us; the launch traced here: 78.8 us
  Pallas kernels  77 us (96%)
  local copies, waits for them, and re-layouts  1.84 us (2%)
    pallas_call x1, Pallas kernels, body(): pl.pallas_call(kernel, out_shape=jax.ShapeDtypeStruct((W, 2 * W), F32), i...  77 us
    unnamed x3, local copies, waits for them, and re-layouts  1.84 us

profile of v3, /device:TPU:30, one launch (start us, length us, event | category | flops | bytes accessed | tf_op | source)
XLA Modules:
  0.0 78.8 jit_solution(8258099833523934606)
XLA Ops:
  0.0 0.0 copy-start
  0.0 1.0 %copy-done = f32[512,256]{1,0:T(8,128)S(1)} copy-done((f32[512,256]{1,0:T(8,128)S(1)}, f32[512,256]{1,0:T(8,128)}, u32[]{:S(2)}) %copy-start) | copy-done | bytes 524312
  1.0 77.0 %shard_map.17 = f32[256,512]{1,0:T(8,128)S(1)} custom-call(f32[512,256]{1,0:T(8,128)S(1)} %copy-done), custom_call_target="tpu_custom_call" | custom-call | flops 3422552064 | bytes 1048576 | tf_op jit(solution)/shard_map/pallas_call | solution.py:374
  78.0 0.8 %copy.3 = f32[256,512]{1,0:T(8,128)} copy(f32[256,512]{1,0:T(8,128)S(1)} %shard_map.17) | data formatting | bytes 1048576
Async XLA Ops:
  0.0 1.0 %copy-start = (f32[512,256]{1,0:T(8,128)S(1)}, f32[512,256]{1,0:T(8,128)}, u32[]{:S(2)}) copy-start(f32[512,256]{1,0:T(8,128)} %x_ref.1) | copy-start | bytes 1572868

commit v4 on v3

--- a/solution.py
+++ b/solution.py
@@ -15,15 +15,15 @@
 NP = 2
 KP = K // NP
 F32, BF16 = jnp.float32, jnp.bfloat16
-STEPS = ((1, 0), (2, 0), (3, 0), (1, 1), (4, 0), (2, 1), (3, 1), (4, 1))
+STEPS = ((1, 0), (1, 1), (2, 0), (2, 1), (3, 0), (4, 0), (3, 1), (4, 1))
 ORDER = (
-    "H", "Y0", "R0", "Y1", "M00", "M01", "R3", "M30", "P0", "F01", "R1", "M10", "O10", "O00", "F30", "F00",
-    "F10", "M11", "S10", "P1", "O30", "M31", "O11", "O01", "O31", "R5", "S00", "M50", "F50", "O50", "F11",
-    "M51", "S01", "O51", "R2", "R4", "M20", "F51", "S30", "M21", "O20", "G10", "M40", "G00", "S51", "F21",
-    "O21", "F31", "M41", "O40", "F40", "R6", "O41", "M60", "S21", "F41", "R7", "F20", "G51", "S40", "M61",
-    "M70", "O70", "O60", "S41", "G21", "S20", "F70", "F60", "S50", "G40", "S60", "M71", "G30", "F61", "O61",
-    "O71", "G01", "G20", "S31", "G41", "S70", "G60", "S11", "G50", "F71", "S71", "S61", "G70", "G11", "G61",
-    "G31", "G71",
+    "H", "R0", "Y0", "M00", "O00", "F00", "Y1", "M01", "O01", "F01", "R1", "M10", "O10", "F10", "S00", "M11",
+    "O11", "F11", "S01", "R2", "P0", "M20", "O20", "F20", "S10", "M21", "O21", "F21", "S11", "R3", "M30",
+    "O30", "F30", "S20", "G00", "M31", "O31", "F31", "S21", "G01", "R4", "P1", "M40", "O40", "F40", "S30",
+    "G10", "M41", "O41", "F41", "S31", "G11", "R5", "M50", "O50", "F50", "S40", "G20", "M51", "O51", "F51",
+    "S41", "G21", "R6", "M60", "O60", "F60", "S50", "G30", "M61", "O61", "F61", "S51", "G31", "R7", "M70",
+    "O70", "F70", "S60", "G40", "M71", "O71", "F71", "S61", "G41", "G50", "G51", "S70", "G60", "S71", "G61",
+    "G70", "G71",
 )
 
 

time: 80.1 us -> 78.9 us (0.985); the launches traced: 78.8 us -> 78.8 us
  no operation moved by 1% of the time
where the time goes in v4:
time: 78.9 us; the launch traced here: 78.8 us
  Pallas kernels  77 us (98%)
  local copies, waits for them, and re-layouts  1.84 us (2%)
    pallas_call x1, Pallas kernels, body(): pl.pallas_call(kernel, out_shape=jax.ShapeDtypeStruct((W, 2 * W), F32), i...  77 us
    unnamed x3, local copies, waits for them, and re-layouts  1.84 us

profile of v4, /device:TPU:30, one launch (start us, length us, event | category | flops | bytes accessed | tf_op | source)
XLA Modules:
  0.0 78.8 jit_solution(12437331623761056912)
XLA Ops:
  0.0 0.0 copy-start
  0.0 1.0 %copy-done = f32[512,256]{1,0:T(8,128)S(1)} copy-done((f32[512,256]{1,0:T(8,128)S(1)}, f32[512,256]{1,0:T(8,128)}, u32[]{:S(2)}) %copy-start) | copy-done | bytes 524312
  1.0 77.0 %shard_map.17 = f32[256,512]{1,0:T(8,128)S(1)} custom-call(f32[512,256]{1,0:T(8,128)S(1)} %copy-done), custom_call_target="tpu_custom_call" | custom-call | flops 3422552064 | bytes 1048576 | tf_op jit(solution)/shard_map/pallas_call | solution.py:374
  78.0 0.8 %copy.3 = f32[256,512]{1,0:T(8,128)} copy(f32[256,512]{1,0:T(8,128)S(1)} %shard_map.17) | data formatting | bytes 1048576
Async XLA Ops:
  0.0 1.0 %copy-start = (f32[512,256]{1,0:T(8,128)S(1)}, f32[512,256]{1,0:T(8,128)}, u32[]{:S(2)}) copy-start(f32[512,256]{1,0:T(8,128)} %x_ref.1) | copy-start | bytes 1572868

commit v5 on v4

--- a/solution.py
+++ b/solution.py
@@ -212,18 +212,20 @@
             device(yh=s // 4, yl=yl2),
         )
 
-    def to_y(h, s, p, act):
+    def to_y(h, s, p, act, only=None):
         for yl2 in range(2):
             away = jnp.logical_or(s // 4 != yh, yl2 != yl)
             wanted = (yl + yl2 + s) % 2 == c
 
-            @pl.when(away)
-            def _():
-                act(y_copy(h, s, yl2, p, 0))
-
-            @pl.when(jnp.logical_and(away, wanted))
-            def _():
-                act(y_copy(h, s, yl2, p, 1))
+            if only != 1:
+                @pl.when(away)
+                def _():
+                    act(y_copy(h, s, yl2, p, 0))
+
+            if only != 0:
+                @pl.when(jnp.logical_and(away, wanted))
+                def _():
+                    act(y_copy(h, s, yl2, p, 1))
 
     def collect(h, s, p):
         @pl.when(role(s) == 0)
@@ -236,7 +238,7 @@
                         f_rs.at[h, s // 4, q, p, t], device(x=x_right),
                     ).wait_recv()
                 part[h, s, p, t] = part[h, s, p, t] + full_in[h, s // 4, 0, p, t] + full_in[h, s // 4, 1, p, t]
-            to_y(h, s, p, lambda copy: copy.start())
+                to_y(h, s, p, lambda copy: copy.start(), t)
 
             @pl.when(s // 4 == yh)
             def _():

time: 78.9 us -> 78 us (0.989)
  Pallas kernels: 77 us -> 75.6 us
    pallas_call x1, Pallas kernels: 77 us -> 75.6 us  [body(): pl.pallas_call(kernel, out_shape=jax.ShapeDtypeStruct((W, 2 * W), F32), i...]
where the time goes in v5:
time: 78 us; the launch traced here: 77.4 us
  Pallas kernels  75.6 us (97%)
  local copies, waits for them, and re-layouts  1.84 us (2%)
    pallas_call x1, Pallas kernels, body(): pl.pallas_call(kernel, out_shape=jax.ShapeDtypeStruct((W, 2 * W), F32), i...  75.6 us
    unnamed x3, local copies, waits for them, and re-layouts  1.84 us

profile of v5, /device:TPU:30, one launch (start us, length us, event | category | flops | bytes accessed | tf_op | source)
XLA Modules:
  0.0 77.4 jit_solution(8453628521935129669)
XLA Ops:
  0.0 0.0 copy-start
  0.0 1.0 %copy-done = f32[512,256]{1,0:T(8,128)S(1)} copy-done((f32[512,256]{1,0:T(8,128)S(1)}, f32[512,256]{1,0:T(8,128)}, u32[]{:S(2)}) %copy-start) | copy-done | bytes 524312
  1.0 75.6 %shard_map.17 = f32[256,512]{1,0:T(8,128)S(1)} custom-call(f32[512,256]{1,0:T(8,128)S(1)} %copy-done), custom_call_target="tpu_custom_call" | custom-call | flops 3422552064 | bytes 1048576 | tf_op jit(solution)/shard_map/pallas_call | solution.py:376
  76.6 0.8 %copy.3 = f32[256,512]{1,0:T(8,128)} copy(f32[256,512]{1,0:T(8,128)S(1)} %shard_map.17) | data formatting | bytes 1048576
Async XLA Ops:
  0.0 1.0 %copy-start = (f32[512,256]{1,0:T(8,128)S(1)}, f32[512,256]{1,0:T(8,128)}, u32[]{:S(2)}) copy-start(f32[512,256]{1,0:T(8,128)} %x_ref.1) | copy-start | bytes 1572868
